TPU v7x, 256 devices: a whole 4x4x8 slice. The times are simulated.
256 devices in a mesh: dp: 2 (over core), head: 8 (over x, z_lo), ctx: 16 (over y, z_hi).
Axes of the slice: x: 4, y: 4, z: 8 (z_hi: 4, z_lo: 2; z = z_hi * 2 + z_lo), core: 2. Of those that a mesh axis runs over, the one named last changes fastest.
Arguments:
- query_states: bfloat16 [2, 16384, 32, 128], P('dp', 'ctx', 'head'), may hold values from -6 to 6
- key_states: bfloat16 [2, 16384, 8, 128], P('dp', 'ctx', 'head'), may hold values from -6 to 6
- value_states: bfloat16 [2, 16384, 8, 128], P('dp', 'ctx', 'head'), may hold values from -12 to 12
- gate_values: float32 [32], P('head'), may hold values from 0.1 to 0.9
- head_flags: int32 [32], P('head'), may hold values from 0 to 1, as said below
- output_grad: bfloat16 [2, 16384, 32, 128], P('dp', 'ctx', 'head'), may hold values from -16 to 16
Outputs:
- blended: bfloat16 [2, 16384, 32, 128], P('dp', 'ctx', 'head')
- gate_grad: float32 [32], replicated
Inputs may be any that keep to these rules, and one draw needn't show every extreme that they name: `head_flags`: exactly 1 of the 4 query heads of each key-value head have flag 1.
All inputs are finite; a program needn't handle non-finite values.
Results may differ from a plain program's by a relative error of at most 0.005.
Values may be sent and summed in bfloat16 or wider, within the bound.
No kernel may reach another device: no remote copies, remote signals or barrier semaphores. Data moves between devices by JAX's collectives and lax.ppermute only.
A program may use at most 64 MiB of HBM per device.

v0:
```python
import math
import jax
import jax.numpy as jnp
from jax import lax
from jax.sharding import PartitionSpec as P

RET = 1
SINK = 64
WINDOW = 2048


def from_behind(block, axis, distance):
    devices = range(lax.axis_size(axis))
    route = [(i - distance, i) for i in devices if i - distance in devices]
    return lax.ppermute(block, axis, route)


def empty_state(row_count, groups, heads, width):
    return (
        jnp.full((row_count, groups, heads), -jnp.inf, jnp.float32),
        jnp.zeros((row_count, groups, heads), jnp.float32),
        jnp.zeros((row_count, groups, heads, width), jnp.float32),
    )


def block_update(carried, query_block, key_rows, value_rows, allowed):
    running_max, running_sum, running_acc = carried
    scaling = 1.0 / math.sqrt(query_block.shape[-1])
    scores = (
        jnp.einsum("rgeh,kgh->rgek", query_block, key_rows, preferred_element_type=jnp.float32)
        * scaling
    )
    visible = allowed[:, None, None, :]
    scores = jnp.where(visible, scores, -jnp.inf)
    newest = jnp.maximum(running_max, jnp.max(scores, axis=-1))
    anchor = jnp.where(newest == -jnp.inf, 0.0, newest)
    factor = jnp.exp(running_max - anchor)
    weights = jnp.where(visible, jnp.exp(scores - anchor[..., None]), 0.0)
    running_sum = running_sum * factor + jnp.sum(weights, axis=-1)
    update = jnp.einsum(
        "rgek,kgh->rgeh",
        weights.astype(jnp.bfloat16),
        value_rows,
        preferred_element_type=jnp.float32,
    )
    running_acc = running_acc * factor[..., None] + update
    return (newest, running_sum, running_acc)


def sweep_blocks(carried, queries, positions, key_rows, value_rows, key_first, needed, allowed_fn):
    row_count = queries.shape[0]
    key_count = key_rows.shape[0]
    row_block = math.gcd(row_count, 512)
    key_block = math.gcd(key_count, 512)
    key_steps = key_count // key_block
    total_steps = row_count // row_block * key_steps

    def visit_block(counter, current):
        row_at = counter // key_steps * row_block
        key_at = counter % key_steps * key_block
        row_pos = lax.dynamic_slice_in_dim(positions, row_at, row_block)
        key_pos = key_first + key_at + jnp.arange(key_block, dtype=jnp.int32)

        def compute(present):
            portion = tuple(
                (lax.dynamic_slice_in_dim(member, row_at, row_block) for member in present)
            )
            renewed = block_update(
                portion,
                lax.dynamic_slice_in_dim(queries, row_at, row_block),
                lax.dynamic_slice_in_dim(key_rows, key_at, key_block),
                lax.dynamic_slice_in_dim(value_rows, key_at, key_block),
                allowed_fn(row_pos[:, None], key_pos[None, :]),
            )
            return tuple(
                (
                    lax.dynamic_update_slice_in_dim(member, fresh_part, row_at, 0)
                    for member, fresh_part in zip(present, renewed)
                )
            )

        def unchanged(present):
            return present

        return lax.cond(
            needed(row_pos[0], row_pos[row_block - 1], key_pos[0], key_pos[key_block - 1]),
            compute,
            unchanged,
            current,
        )

    return lax.fori_loop(0, total_steps, visit_block, carried)


def causal_needed(row_low, row_high, key_low, key_high):
    return key_low <= row_high


def causal_allowed(row_pos, key_pos):
    return key_pos <= row_pos


def window_needed(row_low, row_high, key_low, key_high):
    return (key_low <= row_high) & (key_high > row_low - WINDOW)


def window_allowed(row_pos, key_pos):
    return (key_pos >= 0) & (key_pos <= row_pos) & (row_pos - key_pos < WINDOW)


def sinks_needed(row_low, row_high, key_low, key_high):
    return (key_low < SINK) & (row_high - key_low >= WINDOW)


def sinks_allowed(row_pos, key_pos):
    return (key_pos < SINK) & (key_pos <= row_pos) & (row_pos - key_pos >= WINDOW)


def on_device(query_states, key_states, value_states, gate_values, head_flags, output_grad):
    tok_rows = query_states.shape[1]
    groups = key_states.shape[2]
    head_dim = key_states.shape[3]
    per_group = query_states.shape[2] // groups
    ctx_count = lax.axis_size("ctx")
    ctx_index = lax.axis_index("ctx")
    queries = query_states[0].reshape(tok_rows, groups, per_group, head_dim)
    stacked = jnp.stack([key_states[0], value_states[0]])
    marked = head_flags.reshape(groups, per_group)
    ordinal = jnp.cumsum(marked, axis=1) - 1
    slot_ids = jnp.arange(RET, dtype=jnp.int32)
    picker = ((marked[:, None, :] == 1) & (ordinal[:, None, :] == slot_ids[None, :, None])).astype(
        jnp.float32
    )
    chosen = jnp.einsum(
        "gre,tgeh->tgrh", picker.astype(jnp.bfloat16), queries, preferred_element_type=jnp.float32
    ).astype(jnp.bfloat16)
    own_pos = ctx_index * tok_rows + jnp.arange(tok_rows, dtype=jnp.int32)
    full_state = empty_state(tok_rows, groups, RET, head_dim)
    near_state = empty_state(tok_rows, groups, per_group, head_dim)
    portion = lax.all_gather(stacked, "ctx", axis=1, tiled=True)
    start = jnp.int32(0)
    full_now = sweep_blocks(
        full_state, chosen, own_pos, portion[0], portion[1], start, causal_needed, causal_allowed
    )
    head_rows = min(SINK, portion.shape[1])
    sink_part = portion[:, :head_rows]

    def with_sinks(present):
        return sweep_blocks(
            present,
            queries,
            own_pos,
            sink_part[0],
            sink_part[1],
            start,
            sinks_needed,
            sinks_allowed,
        )

    def without_sinks(present):
        return present

    near_now = lax.cond(start < SINK, with_sinks, without_sinks, near_state)
    near_state = near_now
    reach_depth = min((WINDOW - 1) // tok_rows + 1, ctx_count - 1)
    earlier = [from_behind(stacked, "ctx", distance) for distance in range(reach_depth, 0, -1)]
    near_keys = jnp.concatenate(earlier + [stacked], axis=1)
    near_state = sweep_blocks(
        near_state,
        queries,
        own_pos,
        near_keys[0],
        near_keys[1],
        (ctx_index - reach_depth) * tok_rows,
        window_needed,
        window_allowed,
    )
    full_out = full_now[2] / full_now[1][..., None]
    near_out = near_state[2] / near_state[1][..., None]
    full_heads = jnp.einsum("gre,tgrh->tgeh", picker, full_out, precision=lax.Precision.HIGHEST)
    gate_cols = gate_values.reshape(groups, per_group)[None, :, :, None]
    retrieval = (marked == 1)[None, :, :, None]
    mixed = jnp.where(retrieval, gate_cols * full_heads + (1.0 - gate_cols) * near_out, near_out)
    blended = mixed.astype(jnp.bfloat16).reshape(1, tok_rows, groups * per_group, head_dim)
    grad_rows = output_grad[0].reshape(tok_rows, groups, per_group, head_dim).astype(jnp.float32)
    local_terms = jnp.sum(grad_rows * (full_heads - near_out), axis=(0, 3)) * marked.astype(
        jnp.float32
    )
    heads_dev = groups * per_group
    padded = lax.dynamic_update_slice_in_dim(
        jnp.zeros((heads_dev * lax.axis_size("head"),), jnp.float32),
        local_terms.reshape(heads_dev),
        lax.axis_index("head") * heads_dev,
        0,
    )
    totals = lax.psum(padded, ("dp", "head", "ctx"))
    normalizer = 1.0 / math.sqrt(
        lax.axis_size("dp") * query_states.shape[0] * tok_rows * ctx_count * head_dim
    )
    return (blended, totals * normalizer)


def solution(mesh):
    return jax.shard_map(
        on_device,
        mesh=mesh,
        in_specs=(
            P("dp", "ctx", "head", None),
            P("dp", "ctx", "head", None),
            P("dp", "ctx", "head", None),
            P("head"),
            P("head"),
            P("dp", "ctx", "head", None),
        ),
        out_specs=(P("dp", "ctx", "head", None), P()),
        check_vma=False,
    )
```

profile of v0, /device:TPU:1, one launch (start us, length us, event | category | flops | bytes accessed | tf_op | source)
XLA Modules:
  0.0 829.5 jit_solution(2054756737701288816)
XLA Ops:
  10.1 5.8 collective-permute-start.1
  15.9 7.8 collective-permute-start
  31.2 24.1 %collective-permute-done = bf16[2,1024,1,128]{3,1,2,0:T(8,128)(2,1)} collective-permute-done((bf16[2,1024,1,128]{3,1,2,0:T(8,128)(2,1)}, bf16[2,1024,1,128]{3,1,2,0:T(8,128)(2,1)}, u32[]{:S(2)}, u32[]{:S(2)}) %collective-permute-start) | collective-permute-done | bytes 524320 | tf_op jit(solution)/shard_map/ppermute | solution.py:15
  58.6 96.1 %all-gather.2.cloned.1.call-done = bf16[2,16384,1,128]{3,1,2,0:T(8,128)(2,1)} async-done(((bf16[2,1024,1,128]{3,1,2,0:T(8,128)(2,1)}), bf16[2,16384,1,128]{3,1,2,0:T(8,128)(2,1)}) %all-gather.2.cloned.1.call-update) | async-done | bytes 8388624 | tf_op jit(solution)/shard_map/all_gather | solution.py:140
  154.6 5.7 slice_bitcast_fusion
  160.4 183.1 %while.58 = (s32[]{:T(128)}, f32[1024,1,1]{0,2,1:T(1,128)S(1)}, f32[1024,1,1]{0,2,1:T(1,128)S(1)}, f32[1024,1,1,128]{0,3,2,1:T(8,128)S(1)}, s32[1024]{0:T(1024)S...) while((s32[]{:T(128)}, f32[1024,1,1]{0,2,1:T(1,128)S(1)}, ...), condition=%wide.region_6.7_spmd, body=%wide.region_1.6_spmd.sunk | while | flops 137498128 | bytes 4645472 | solution.py:92
  163.1 3.7 conditional.6
  252.9 3.6 conditional.6
  259.2 3.6 conditional.6
  350.4 158.5 %while.60 = (s32[]{:T(128)}, f32[1024,1,4]{0,2,1:T(4,128)S(1)}, f32[1024,1,4]{0,2,1:T(4,128)S(1)}, f32[1024,1,4,128]{0,3,2,1:T(8,128)}, s32[]{:T(128)}, /*index=...) while((s32[]{:T(128)}, f32[1024,1,4]{0,2,1:T(4,128)S(1)}, ...), condition=%wide.region_18.19_spmd, body=%wide.region_13.18_spmd.sunk | while | flops 552356864 | bytes 27178672 | solution.py:92
  353.4 12.6 %conditional.8 = ((f32[1024,1,4]{0,2,1:T(4,128)S(1)}, f32[1024,1,4]{0,2,1:T(4,128)S(1)}, f32[1024,1,4,128]{0,3,2,1:T(8,128)})) conditional(s32[]{:T(128)} %bitcast.205, (f32[1024,1,4]{0,2,1:T(4,128)S(1)}, f32[1024,1,4]{0,2,1:T(4,128)S(1)}, f32[1024,1,4,128]{0,3,2,1:T(8,128)}) %tuple.164, (s32[]{:T(128)}, f32[1024,1,4]{0,2,1:T(4,128)S(1)}, ...), branch_computations={%region_14.14_spmd, %region_15.17_spmd} | conditional | flops 552356352 | bytes 27172004 | solution.py:85
  360.3 5.7 dynamic_update_slice.31
  369.1 12.6 %conditional.8 = ((f32[1024,1,4]{0,2,1:T(4,128)S(1)}, f32[1024,1,4]{0,2,1:T(4,128)S(1)}, f32[1024,1,4,128]{0,3,2,1:T(8,128)})) conditional(s32[]{:T(128)} %bitcast.205, (f32[1024,1,4]{0,2,1:T(4,128)S(1)}, f32[1024,1,4]{0,2,1:T(4,128)S(1)}, f32[1024,1,4,128]{0,3,2,1:T(8,128)}) %tuple.164, (s32[]{:T(128)}, f32[1024,1,4]{0,2,1:T(4,128)S(1)}, ...), branch_computations={%region_14.14_spmd, %region_15.17_spmd} | conditional | flops 552356352 | bytes 27172004 | solution.py:85
  376.0 5.7 dynamic_update_slice.31
  384.8 12.6 %conditional.8 = ((f32[1024,1,4]{0,2,1:T(4,128)S(1)}, f32[1024,1,4]{0,2,1:T(4,128)S(1)}, f32[1024,1,4,128]{0,3,2,1:T(8,128)})) conditional(s32[]{:T(128)} %bitcast.205, (f32[1024,1,4]{0,2,1:T(4,128)S(1)}, f32[1024,1,4]{0,2,1:T(4,128)S(1)}, f32[1024,1,4,128]{0,3,2,1:T(8,128)}) %tuple.164, (s32[]{:T(128)}, f32[1024,1,4]{0,2,1:T(4,128)S(1)}, ...), branch_computations={%region_14.14_spmd, %region_15.17_spmd} | conditional | flops 552356352 | bytes 27172004 | solution.py:85
  391.6 5.7 dynamic_update_slice.31
  400.4 12.6 %conditional.8 = ((f32[1024,1,4]{0,2,1:T(4,128)S(1)}, f32[1024,1,4]{0,2,1:T(4,128)S(1)}, f32[1024,1,4,128]{0,3,2,1:T(8,128)})) conditional(s32[]{:T(128)} %bitcast.205, (f32[1024,1,4]{0,2,1:T(4,128)S(1)}, f32[1024,1,4]{0,2,1:T(4,128)S(1)}, f32[1024,1,4,128]{0,3,2,1:T(8,128)}) %tuple.164, (s32[]{:T(128)}, f32[1024,1,4]{0,2,1:T(4,128)S(1)}, ...), branch_computations={%region_14.14_spmd, %region_15.17_spmd} | conditional | flops 552356352 | bytes 27172004 | solution.py:85
  407.3 5.7 dynamic_update_slice.31
  416.1 12.6 %conditional.8 = ((f32[1024,1,4]{0,2,1:T(4,128)S(1)}, f32[1024,1,4]{0,2,1:T(4,128)S(1)}, f32[1024,1,4,128]{0,3,2,1:T(8,128)})) conditional(s32[]{:T(128)} %bitcast.205, (f32[1024,1,4]{0,2,1:T(4,128)S(1)}, f32[1024,1,4]{0,2,1:T(4,128)S(1)}, f32[1024,1,4,128]{0,3,2,1:T(8,128)}) %tuple.164, (s32[]{:T(128)}, f32[1024,1,4]{0,2,1:T(4,128)S(1)}, ...), branch_computations={%region_14.14_spmd, %region_15.17_spmd} | conditional | flops 552356352 | bytes 27172004 | solution.py:85
  423.0 5.7 dynamic_update_slice.31
  438.0 11.7 %conditional.8 = ((f32[1024,1,4]{0,2,1:T(4,128)S(1)}, f32[1024,1,4]{0,2,1:T(4,128)S(1)}, f32[1024,1,4,128]{0,3,2,1:T(8,128)})) conditional(s32[]{:T(128)} %bitcast.205, (f32[1024,1,4]{0,2,1:T(4,128)S(1)}, f32[1024,1,4]{0,2,1:T(4,128)S(1)}, f32[1024,1,4,128]{0,3,2,1:T(8,128)}) %tuple.164, (s32[]{:T(128)}, f32[1024,1,4]{0,2,1:T(4,128)S(1)}, ...), branch_computations={%region_14.14_spmd, %region_15.17_spmd} | conditional | flops 552356352 | bytes 27172004 | solution.py:85
  444.7 5.0 dynamic_update_slice.31
  452.8 11.8 %conditional.8 = ((f32[1024,1,4]{0,2,1:T(4,128)S(1)}, f32[1024,1,4]{0,2,1:T(4,128)S(1)}, f32[1024,1,4,128]{0,3,2,1:T(8,128)})) conditional(s32[]{:T(128)} %bitcast.205, (f32[1024,1,4]{0,2,1:T(4,128)S(1)}, f32[1024,1,4]{0,2,1:T(4,128)S(1)}, f32[1024,1,4,128]{0,3,2,1:T(8,128)}) %tuple.164, (s32[]{:T(128)}, f32[1024,1,4]{0,2,1:T(4,128)S(1)}, ...), branch_computations={%region_14.14_spmd, %region_15.17_spmd} | conditional | flops 552356352 | bytes 27172004 | solution.py:85
  459.5 5.0 dynamic_update_slice.31
  467.6 11.7 %conditional.8 = ((f32[1024,1,4]{0,2,1:T(4,128)S(1)}, f32[1024,1,4]{0,2,1:T(4,128)S(1)}, f32[1024,1,4,128]{0,3,2,1:T(8,128)})) conditional(s32[]{:T(128)} %bitcast.205, (f32[1024,1,4]{0,2,1:T(4,128)S(1)}, f32[1024,1,4]{0,2,1:T(4,128)S(1)}, f32[1024,1,4,128]{0,3,2,1:T(8,128)}) %tuple.164, (s32[]{:T(128)}, f32[1024,1,4]{0,2,1:T(4,128)S(1)}, ...), branch_computations={%region_14.14_spmd, %region_15.17_spmd} | conditional | flops 552356352 | bytes 27172004 | solution.py:85
  474.3 5.0 dynamic_update_slice.31
  482.4 11.8 %conditional.8 = ((f32[1024,1,4]{0,2,1:T(4,128)S(1)}, f32[1024,1,4]{0,2,1:T(4,128)S(1)}, f32[1024,1,4,128]{0,3,2,1:T(8,128)})) conditional(s32[]{:T(128)} %bitcast.205, (f32[1024,1,4]{0,2,1:T(4,128)S(1)}, f32[1024,1,4]{0,2,1:T(4,128)S(1)}, f32[1024,1,4,128]{0,3,2,1:T(8,128)}) %tuple.164, (s32[]{:T(128)}, f32[1024,1,4]{0,2,1:T(4,128)S(1)}, ...), branch_computations={%region_14.14_spmd, %region_15.17_spmd} | conditional | flops 552356352 | bytes 27172004 | solution.py:85
  489.1 5.0 dynamic_update_slice.31
  497.2 11.7 %conditional.8 = ((f32[1024,1,4]{0,2,1:T(4,128)S(1)}, f32[1024,1,4]{0,2,1:T(4,128)S(1)}, f32[1024,1,4,128]{0,3,2,1:T(8,128)})) conditional(s32[]{:T(128)} %bitcast.205, (f32[1024,1,4]{0,2,1:T(4,128)S(1)}, f32[1024,1,4]{0,2,1:T(4,128)S(1)}, f32[1024,1,4,128]{0,3,2,1:T(8,128)}) %tuple.164, (s32[]{:T(128)}, f32[1024,1,4]{0,2,1:T(4,128)S(1)}, ...), branch_computations={%region_14.14_spmd, %region_15.17_spmd} | conditional | flops 552356352 | bytes 27172004 | solution.py:85
  503.9 5.0 dynamic_update_slice.31
  511.2 6.3 fusion.69
  517.7 304.5 %psum.7 = f32[32]{0:T(128)S(1)} all-reduce(f32[32]{0:T(128)S(1)} %multiply_dynamic-update-slice_fusion), channel_id=1, replica_groups=mesh['dp'=2,'head'=8,'ctx'=16] {'dp','head','ctx'}, use_global_device_ids=true, to_apply=%region_20.21 | all-reduce | flops 32 | bytes 256 | tf_op jit(solution)/shard_map/psum | solution.py:196
  (552 shorter events, 196.3 us)
Async XLA Ops:
  7.2 20.2 %copy-start.4 = (bf16[1,1024,4,128]{3,2,1,0:T(4,128)(2,1)S(1)}, bf16[1,1024,4,128]{3,2,1,0:T(4,128)(2,1)}, u32[]{:S(2)}) copy-start(bf16[1,1024,4,128]{3,2,1,0:T(4,128)(2,1)} %param.18) | copy-start | bytes 3145732
  7.2 147.5 %all-gather.2.cloned.1.call-start = ((), (), s32[]{:S(2)}) async-start(), calls=%async_computation | async-start | bytes 8912896 | tf_op jit(solution)/shard_map/all_gather | solution.py:140
  9.3 0.8 copy-start.1
  10.1 21.1 %collective-permute-start.1 = (bf16[2,1024,1,128]{3,1,2,0:T(8,128)(2,1)}, bf16[2,1024,1,128]{3,1,2,0:T(8,128)(2,1)S(1)}, u32[]{:S(2)}, u32[]{:S(2)}) collective-permute-start(bf16[2,1024,1,128]{3,1,2,0:T(8,128)(2,1)} %copy-done.1), channel_id=1, source_target_pairs={{0,1},{1,2},{2,3},{3,4},{4,5},{5,6},{6,7},{7,8},{8,9},{9,10},{10,1... | collective-permute-start | bytes 1572872 | tf_op jit(solution)/shard_map/ppermute | solution.py:15
  15.9 39.4 %collective-permute-start = (bf16[2,1024,1,128]{3,1,2,0:T(8,128)(2,1)}, bf16[2,1024,1,128]{3,1,2,0:T(8,128)(2,1)}, u32[]{:S(2)}, u32[]{:S(2)}) collective-permute-start(bf16[2,1024,1,128]{3,1,2,0:T(8,128)(2,1)} %copy-done.1), channel_id=1, source_target_pairs={{0,2},{1,3},{2,4},{3,5},{4,6},{5,7},{6,8},{7,9},{8,10},{9,11},{10,... | collective-permute-start | bytes 1572872 | tf_op jit(solution)/shard_map/ppermute | solution.py:15
  25.8 29.4 %copy-start.2 = (bf16[2,1024,1,128]{3,1,2,0:T(8,128)(2,1)S(1)}, bf16[2,1024,1,128]{3,1,2,0:T(8,128)(2,1)}, u32[]{:S(2)}) copy-start(bf16[2,1024,1,128]{3,1,2,0:T(8,128)(2,1)} %copy-done.1) | copy-start | bytes 1572868
  355.7 1.6 copy-start
  371.4 1.6 copy-start
  387.0 1.6 copy-start
  402.7 1.6 copy-start
  418.4 1.6 copy-start
  440.3 1.6 copy-start
  455.1 1.6 copy-start
  469.9 1.6 copy-start
  484.7 1.6 copy-start
  499.5 1.6 copy-start
  508.9 2.3 copy-start.3
  508.9 2.3 copy-start.6
  511.2 6.4 copy-start.5
Sparse Core Ops, SparseCore 0:
  10.5 144.0 all-gather.1
where the time goes:
time: 836 us; the launch traced here: 829 us
  blocking collectives  304 us (36%)
  local copies, waits for them, and re-layouts  177 us (21%)
  waiting for transfers between devices  123 us (15%)
  loops' own time  119 us (14%)
  matrix products  50 us (6%)
  other arithmetic  27.9 us (3%)
  between operations  14.2 us (2%)
  starting transfers between devices  13.6 us (2%)
    psum x1, blocking collectives, on_device(): totals = lax.psum(padded, ('dp', 'head', 'ctx'))  304 us
    another operation x3, loops' own time, sweep_blocks(): return lax.fori_loop(0, total_steps, visit_block, carried)  117 us
    all_gather x1, waiting for transfers between devices, on_device(): portion = lax.all_gather(stacked, 'ctx', axis=1, tiled=True)  96.1 us
    dynamic_update_slice x39, local copies, waits for them, and re-layouts, compute(): lax.dynamic_update_slice_in_dim(member, fresh_part, row_at, 0)  60.7 us
    slice x66, local copies, waits for them, and re-layouts, visit_block(): row_pos[row_block - 1]  42.8 us
    slice x64, local copies, waits for them, and re-layouts, visit_block(): key_pos[0]  37.7 us
    ppermute x2, waiting for transfers between devices, from_behind(): return lax.ppermute(block, axis, route)  27.2 us
    dot_general x13, matrix products, block_update(): jnp.einsum('rgek,kgh->rgeh', weights.astype(jnp.bfloat16), value_rows, pr...  26.8 us
  transfers between devices with their start and end apart: 3, of which 3 were waited for; matrix products, arithmetic and copies ran while one was open for 1% of the time, Pallas kernels for 0%

commit v1 on v0

--- a/solution.py
+++ b/solution.py
@@ -193,7 +193,7 @@
         lax.axis_index("head") * heads_dev,
         0,
     )
-    totals = lax.psum(padded, ("dp", "head", "ctx"))
+    totals = jnp.sum(lax.all_gather(padded, ("dp", "head", "ctx")), axis=0)
     normalizer = 1.0 / math.sqrt(
         lax.axis_size("dp") * query_states.shape[0] * tok_rows * ctx_count * head_dim
     )

time: 836 us -> 1420 us (1.70)
  the two profiles are of different devices: /device:TPU:1 before, /device:TPU:36 now
where the time goes in v1:
time: 1420 us; the launch traced here: 1410 us
  blocking collectives  879 us (62%)
  local copies, waits for them, and re-layouts  177 us (12%)
  waiting for transfers between devices  129 us (9%)
  loops' own time  119 us (8%)
  matrix products  50 us (4%)
  other arithmetic  28.1 us (2%)
    all_gather x1, blocking collectives, on_device(): totals = jnp.sum(lax.all_gather(padded, ('dp', 'head', 'ctx')), axis=0)  879 us
    another operation x3, loops' own time, sweep_blocks(): return lax.fori_loop(0, total_steps, visit_block, carried)  117 us
    all_gather x1, waiting for transfers between devices, on_device(): portion = lax.all_gather(stacked, 'ctx', axis=1, tiled=True)  84.6 us
    dynamic_update_slice x39, local copies, waits for them, and re-layouts, compute(): lax.dynamic_update_slice_in_dim(member, fresh_part, row_at, 0)  60.7 us
    ppermute x2, waiting for transfers between devices, from_behind(): return lax.ppermute(block, axis, route)  44.5 us
    slice x66, local copies, waits for them, and re-layouts, visit_block(): row_pos[row_block - 1]  42.8 us
    slice x64, local copies, waits for them, and re-layouts, visit_block(): key_pos[0]  37.7 us
  transfers between devices with their start and end apart: 3, of which 2 were waited for; matrix products, arithmetic and copies ran while one was open for 1% of the time, Pallas kernels for 0%

profile of v1, /device:TPU:36, one launch (start us, length us, event | category | flops | bytes accessed | tf_op | source)
XLA Modules:
  0.0 1409.7 jit_solution(3738678103614482157)
XLA Ops:
  10.1 5.2 collective-permute-start.1
  15.3 7.2 collective-permute-start
  26.9 44.5 %collective-permute-done.1 = bf16[2,1024,1,128]{3,1,2,0:T(8,128)(2,1)S(1)} collective-permute-done((bf16[2,1024,1,128]{3,1,2,0:T(8,128)(2,1)}, bf16[2,1024,1,128]{3,1,2,0:T(8,128)(2,1)S(1)}, u32[]{:S(2)}, u32[]{:S(2)}) %collective-permute-start.1) | collective-permute-done | bytes 524320 | tf_op jit(solution)/shard_map/ppermute | solution.py:15
  74.8 84.6 %all-gather.3.cloned.1.call-done = bf16[2,16384,1,128]{3,1,2,0:T(8,128)(2,1)} async-done(((bf16[2,1024,1,128]{3,1,2,0:T(8,128)(2,1)}), bf16[2,16384,1,128]{3,1,2,0:T(8,128)(2,1)}) %all-gather.3.cloned.1.call-update) | async-done | bytes 8388624 | tf_op jit(solution)/shard_map/all_gather | solution.py:140
  159.4 5.7 slice_bitcast_fusion
  165.2 183.1 %while.58 = (s32[]{:T(128)}, f32[1024,1,1]{0,2,1:T(1,128)S(1)}, f32[1024,1,1]{0,2,1:T(1,128)S(1)}, f32[1024,1,1,128]{0,3,2,1:T(8,128)S(1)}, s32[1024]{0:T(1024)S...) while((s32[]{:T(128)}, f32[1024,1,1]{0,2,1:T(1,128)S(1)}, ...), condition=%wide.region_6.7_spmd, body=%wide.region_1.6_spmd.sunk | while | flops 137498128 | bytes 4645472 | solution.py:92
  167.9 3.7 conditional.6
  257.6 3.6 conditional.6
  264.0 3.6 conditional.6
  355.2 158.5 %while.60 = (s32[]{:T(128)}, f32[1024,1,4]{0,2,1:T(4,128)S(1)}, f32[1024,1,4]{0,2,1:T(4,128)S(1)}, f32[1024,1,4,128]{0,3,2,1:T(8,128)}, s32[]{:T(128)}, /*index=...) while((s32[]{:T(128)}, f32[1024,1,4]{0,2,1:T(4,128)S(1)}, ...), condition=%wide.region_18.19_spmd, body=%wide.region_13.18_spmd.sunk | while | flops 552356864 | bytes 27178672 | solution.py:92
  358.2 12.6 conditional.8
  365.1 5.7 dynamic_update_slice.32
  373.9 12.6 conditional.8
  380.7 5.7 dynamic_update_slice.32
  389.5 12.6 conditional.8
  396.4 5.7 dynamic_update_slice.32
  405.2 12.6 conditional.8
  412.1 5.7 dynamic_update_slice.32
  420.8 12.6 conditional.8
  427.7 5.7 dynamic_update_slice.32
  442.8 11.7 conditional.8
  449.5 5.0 dynamic_update_slice.32
  457.6 11.8 conditional.8
  464.3 5.0 dynamic_update_slice.32
  472.4 11.7 conditional.8
  479.1 5.0 dynamic_update_slice.32
  487.1 11.8 conditional.8
  493.9 5.0 dynamic_update_slice.32
  501.9 11.7 conditional.8
  508.7 5.0 dynamic_update_slice.32
  516.0 6.3 fusion.69
  522.6 879.4 %all-gather = f32[256,1,32]{2,1,0:T(1,128)S(1)} all-gather(f32[1,1,32]{2,1,0:T(1,128)S(1)} %dynamic_update_slice.35), channel_id=1, replica_groups=mesh['dp'=2,'head'=8,'ctx'=16] {'dp','head','ctx'}, dimensions={0}, use_global_device_ids=true | all-gather | bytes 32896 | tf_op jit(solution)/shard_map/all_gather | solution.py:196
  (554 shorter events, 193.7 us)
Async XLA Ops:
  7.2 19.0 %copy-start.4 = (bf16[1,1024,4,128]{3,2,1,0:T(4,128)(2,1)S(1)}, bf16[1,1024,4,128]{3,2,1,0:T(4,128)(2,1)}, u32[]{:S(2)}) copy-start(bf16[1,1024,4,128]{3,2,1,0:T(4,128)(2,1)} %param.18) | copy-start | bytes 3145732
  7.2 152.2 %all-gather.3.cloned.1.call-start = ((), (), s32[]{:S(2)}) async-start(), calls=%async_computation | async-start | bytes 8912896 | tf_op jit(solution)/shard_map/all_gather | solution.py:140
  9.3 0.8 copy-start.1
  10.1 61.4 %collective-permute-start.1 = (bf16[2,1024,1,128]{3,1,2,0:T(8,128)(2,1)}, bf16[2,1024,1,128]{3,1,2,0:T(8,128)(2,1)S(1)}, u32[]{:S(2)}, u32[]{:S(2)}) collective-permute-start(bf16[2,1024,1,128]{3,1,2,0:T(8,128)(2,1)} %copy-done.1), channel_id=1, source_target_pairs={{0,1},{1,2},{2,3},{3,4},{4,5},{5,6},{6,7},{7,8},{8,9},{9,10},{10,1... | collective-permute-start | bytes 1572872 | tf_op jit(solution)/shard_map/ppermute | solution.py:15
  15.3 56.1 %collective-permute-start = (bf16[2,1024,1,128]{3,1,2,0:T(8,128)(2,1)}, bf16[2,1024,1,128]{3,1,2,0:T(8,128)(2,1)}, u32[]{:S(2)}, u32[]{:S(2)}) collective-permute-start(bf16[2,1024,1,128]{3,1,2,0:T(8,128)(2,1)} %copy-done.1), channel_id=1, source_target_pairs={{0,2},{1,3},{2,4},{3,5},{4,6},{5,7},{6,8},{7,9},{8,10},{9,11},{10,... | collective-permute-start | bytes 1572872 | tf_op jit(solution)/shard_map/ppermute | solution.py:15
  24.7 46.8 %copy-start.2 = (bf16[2,1024,1,128]{3,1,2,0:T(8,128)(2,1)S(1)}, bf16[2,1024,1,128]{3,1,2,0:T(8,128)(2,1)}, u32[]{:S(2)}) copy-start(bf16[2,1024,1,128]{3,1,2,0:T(8,128)(2,1)} %copy-done.1) | copy-start | bytes 1572868
  360.5 1.6 copy-start
  376.2 1.6 copy-start
  391.8 1.6 copy-start
  407.5 1.6 copy-start
  423.2 1.6 copy-start
  445.1 1.6 copy-start
  459.9 1.6 copy-start
  474.7 1.6 copy-start
  489.5 1.6 copy-start
  504.2 1.6 copy-start
  513.7 2.3 copy-start.3
  513.7 2.3 copy-start.5
  515.9 6.4 copy-start.6
Sparse Core Ops, SparseCore 0:
  10.5 148.8 all-gather.2
